TPU v7x, 32 devices: a whole 2x2x4 slice. The times are simulated.
32 devices in a mesh: groups: 1, vocab: 32 (over z, y, x, core).
Axes of the slice: x: 2, y: 2, z: 4, core: 2. Of those that a mesh axis runs over, the one named last changes fastest.
Arguments:
- policy_hidden: bfloat16 [512, 5120], P(('groups', 'vocab')), may hold values from -62 to 62
- frozen_hidden: bfloat16 [512, 5120], P(('groups', 'vocab')), may hold values from -62 to 62
- policy_head: bfloat16 [20480, 5120], P('vocab'), may hold values from -2.51557647 to 2.51557647
- frozen_head: bfloat16 [20480, 5120], P('vocab'), may hold values from -2.51557647 to 2.51557647
- actions: int32 [512], P('groups'), may hold values from 0 to 20479
- behavior_logprob: float32 [512], P('groups'), may hold values from -19 to -13
- advantage_sign: int32 [512], P('groups'), may hold values from 0 to 1
- advantage_size: float32 [512], P('groups'), may hold values from 0.2 to 2
- response_mask: int32 [512], P('groups'), may hold values 0 or 1
Outputs:
- hidden_grad: bfloat16 [512, 5120], P(('groups', 'vocab'))
- surrogate_loss: float32 [1], P('groups')
All inputs are finite; a program needn't handle non-finite values.
Results may differ from a plain program's by a relative error of at most 0.0053.
Values may be sent and summed in bfloat16 or wider, within the bound.
A program may use at most 128 MiB of HBM per device.

v0:
```python
import jax
import jax.numpy as jnp
from jax import lax
from jax.sharding import PartitionSpec as P

clip_eps = 0.2
dual_bound = 3.0
kl_weight = 0.1
loss_scale = 16.0


def head_product(rows_block, head):
    return lax.dot_general(
        rows_block, head, (((1,), (1,)), ((), ())), preferred_element_type=jnp.float32
    )


def surrogate(picked_logp, behavior_logprob, advantage_sign, advantage_size):
    advantage = (2 * advantage_sign - 1).astype(jnp.float32) * advantage_size
    ratio = jnp.exp(picked_logp - behavior_logprob)
    clipped = jnp.clip(ratio, 1.0 - clip_eps, 1.0 + clip_eps)
    primary = jnp.maximum(-advantage * ratio, -advantage * clipped)
    objective = jnp.where(advantage < 0, jnp.minimum(primary, -dual_bound * advantage), primary)
    upward = (advantage > 0) & (ratio <= 1.0 + clip_eps)
    downward = (advantage < 0) & (ratio >= 1.0 - clip_eps) & (ratio <= dual_bound)
    slope = jnp.where(upward | downward, -advantage * ratio, jnp.zeros_like(ratio))
    return (objective, slope)


def local_sums(policy_logits, frozen_logits, policy_peak, frozen_peak, chosen):
    policy_exp = jnp.exp(policy_logits - policy_peak[:, None])
    policy_total = jnp.sum(policy_exp, axis=1)
    gap_total = jnp.sum(policy_exp * (policy_logits - frozen_logits), axis=1)
    frozen_total = jnp.sum(jnp.exp(frozen_logits - frozen_peak[:, None]), axis=1)
    picked = jnp.sum(jnp.where(chosen, policy_logits, jnp.zeros_like(policy_logits)), axis=1)
    return (policy_total, gap_total, frozen_total, picked)


def shards(
    policy_hidden,
    frozen_hidden,
    policy_head,
    frozen_head,
    actions,
    behavior_logprob,
    advantage_sign,
    advantage_size,
    response_mask,
):
    own_rows = policy_hidden.shape[0]
    vocab_rows = policy_head.shape[0]
    policy_all, frozen_all = (
        lax.all_gather(policy_hidden, "vocab", axis=0, tiled=True),
        lax.all_gather(frozen_hidden, "vocab", axis=0, tiled=True),
    )
    policy_logits = head_product(policy_all, policy_head)
    frozen_logits = head_product(frozen_all, frozen_head)
    offset = lax.axis_index("vocab") * vocab_rows
    columns = offset + jnp.arange(vocab_rows, dtype=jnp.int32)
    chosen = actions[:, None] == columns[None, :]
    policy_local = jnp.max(policy_logits, axis=1)
    frozen_local = jnp.max(frozen_logits, axis=1)
    policy_peak, frozen_peak = lax.pmax((policy_local, frozen_local), "vocab")
    sums_here = local_sums(policy_logits, frozen_logits, policy_peak, frozen_peak, chosen)
    policy_total, gap_total, frozen_total, picked = lax.psum(
        (sums_here[0], sums_here[1], sums_here[2], sums_here[3]), "vocab"
    )
    policy_lse = policy_peak + jnp.log(policy_total)
    frozen_lse = frozen_peak + jnp.log(frozen_total)
    divergence = gap_total / policy_total - policy_lse + frozen_lse
    objective, slope = surrogate(
        picked - policy_lse, behavior_logprob, advantage_sign, advantage_size
    )
    weight = response_mask.astype(jnp.float32)
    surrogate_loss = jnp.sum(weight * (objective + kl_weight * divergence)).reshape(1)
    policy_prob = jnp.exp(policy_logits - policy_lse[:, None])
    log_gap = policy_logits - frozen_logits - policy_lse[:, None] + frozen_lse[:, None]
    logit_grad = (loss_scale * weight)[:, None] * (
        slope[:, None] * (chosen.astype(jnp.float32) - policy_prob)
        + kl_weight * policy_prob * (log_gap - divergence[:, None])
    )
    logit_grad = logit_grad.astype(jnp.bfloat16)
    partial_grad = jnp.dot(logit_grad, policy_head, preferred_element_type=jnp.float32)
    summed = lax.psum(partial_grad, "vocab")
    hidden_grad = lax.dynamic_slice_in_dim(summed, lax.axis_index("vocab") * own_rows, own_rows, 0)
    return (hidden_grad.astype(jnp.bfloat16), surrogate_loss)


def solution(mesh):
    placed = (
        P(("groups", "vocab"), None),
        P(("groups", "vocab"), None),
        P("vocab", None),
        P("vocab", None),
        P("groups"),
        P("groups"),
        P("groups"),
        P("groups"),
        P("groups"),
    )
    return jax.shard_map(
        shards,
        mesh=mesh,
        in_specs=placed,
        out_specs=(P(("groups", "vocab"), None), P("groups")),
        check_vma=False,
    )
```

profile of v0, /device:TPU:0, one launch (start us, length us, event | category | flops | bytes accessed | tf_op | source)
XLA Modules:
  0.0 432.8 jit_solution(10770974888915463300)
XLA Ops:
  7.2 0.0 all-gather.3.cloned.1.call-start
  7.2 0.7 all-gather.3.cloned.1.call-update
  7.9 0.0 all-gather.5.cloned.1.call-start
  7.9 0.7 all-gather.5.cloned.1.call-update
  8.7 70.2 %all-gather.3.cloned.1.call-done = bf16[512,5120]{1,0:T(8,128)(2,1)} async-done(((bf16[16,5120]{1,0:T(8,128)(2,1)}), bf16[512,5120]{1,0:T(8,128)(2,1)}) %all-gather.3.cloned.1.call-update) | async-done | bytes 5242896 | tf_op jit(solution)/shard_map/all_gather | solution.py:53
  78.9 8.3 %fusion.23 = (f32[512]{0:T(512)S(1)}, f32[512,640]{1,0:T(8,128)S(1)}) fusion(bf16[512,5120]{1,0:T(8,128)(2,1)} %all-gather.3.cloned.1.call-done, bf16[640,5120]{1,0:T(8,128)(2,1)} %param.11), kind=kOutput, calls=%fused_computation.39 | convolution fusion | flops 3355770368 | bytes 13109248 | tf_op jit(solution)/shard_map/dot_general | solution.py:13
  87.2 0.0 copy-start.4
  87.2 58.7 %all-gather.5.cloned.1.call-done = bf16[512,5120]{1,0:T(8,128)(2,1)} async-done(((bf16[16,5120]{1,0:T(8,128)(2,1)}), bf16[512,5120]{1,0:T(8,128)(2,1)}) %all-gather.5.cloned.1.call-update) | async-done | bytes 5242896 | tf_op jit(solution)/shard_map/all_gather | solution.py:54
  145.9 8.3 %fusion.22 = (f32[512]{0:T(512)S(1)}, f32[512,640]{1,0:T(8,128)S(1)}) fusion(bf16[512,5120]{1,0:T(8,128)(2,1)} %all-gather.5.cloned.1.call-done, bf16[640,5120]{1,0:T(8,128)(2,1)} %param.12), kind=kOutput, calls=%fused_computation.38 | convolution fusion | flops 3355770368 | bytes 13109248 | tf_op jit(solution)/shard_map/dot_general | solution.py:13
  154.2 39.7 %all-reduce.1 = (f32[512]{0:T(512)S(1)}, f32[512]{0:T(512)S(1)}) all-reduce(f32[512]{0:T(512)S(1)} %get-tuple-element.17, f32[512]{0:T(512)S(1)} %get-tuple-element.19), channel_id=1, replica_groups=mesh['groups'=1,'vocab'=32] {'vocab'}, use_global_device_ids=true, to_apply=%region_7.8 | all-reduce | flops 1024 | bytes 8192 | tf_op jit(solution)/shard_map/pmax | solution.py:63
  193.9 0.0 copy-done.4
  193.9 0.0 copy-start
  193.9 0.0 copy-start.1
  193.9 0.0 copy-start.2
  193.9 0.0 copy-start.3
  193.9 1.1 multiply_reduce_fusion
  195.0 39.6 %all-reduce = (f32[512]{0:T(512)S(1)}, f32[512]{0:T(512)S(1)}, f32[512]{0:T(512)S(1)}, f32[512]{0:T(512)S(1)}) all-reduce(f32[512]{0:T(512)S(1)} %get-tuple-element.5, f32[512]{0:T(512)S(1)} %get-tuple-element.3, f32[512]{0:T(512)S(1)} %get-tuple-element.2, f32[512]{0:T(512)S(1)} %get-tuple-element.4), channel_id=1, replica_groups=mesh['groups'=1,'vocab'=32] {'vocab'}, use_global_device_ids=true, to_apply=%region_9.10 | all-reduce | flops 2048 | bytes 16384 | tf_op jit(solution)/shard_map/psum | solution.py:65
  234.6 0.0 copy-done
  234.6 0.0 copy-done.1
  234.6 0.0 copy-done.2
  234.6 0.0 copy-done.3
  234.6 0.6 fusion.20
  235.3 10.4 %fusion.7 = f32[512,5120]{1,0:T(8,128)} fusion(bf16[640,5120]{1,0:T(8,128)(2,1)} %param.11, f32[512,640]{1,0:T(8,128)S(1)} %get-tuple-element.20, f32[512]{0:T(512)S(1)} %get-tuple-element.13, f32[512]{0:T(512)S(1)} %get-tuple-element.15, f32[512]{0:T(512)S(1)} %get-tuple-element.14, f32[512]{0:T(512)S(1)} %or_select_fusion, s32[640]{0:T(1024)S(1)} %iota_add_fusion, ...), kind=kOutput, calls=%fused_computation.12 | convolution fusion | flops 3360030720 | bytes 19675648 | tf_op jit(solution)/shard_map/dot_general | solution.py:83
  245.7 178.7 %all-reduce.3 = bf16[512,5120]{1,0:T(8,128)(2,1)} all-reduce(f32[512,5120]{1,0:T(8,128)} %fusion.7), channel_id=1, replica_groups=mesh['groups'=1,'vocab'=32] {'vocab'}, use_global_device_ids=true, to_apply=%region_12.13 | all-reduce | flops 2621440 | bytes 15728640 | tf_op jit(solution)/shard_map/psum | solution.py:84
  424.4 1.6 dynamic-slice_convert_fusion
  (2 shorter events, 0.0 us)
Async XLA Ops:
  7.2 71.7 %all-gather.3.cloned.1.call-start = ((), (), s32[]{:S(2)}) async-start(), calls=%async_computation | async-start | bytes 5406720 | tf_op jit(solution)/shard_map/all_gather | solution.py:53
  7.9 138.0 %all-gather.5.cloned.1.call-start = ((), (), s32[]{:S(2)}) async-start(), calls=%async_computation.1 | async-start | bytes 5406720 | tf_op jit(solution)/shard_map/all_gather | solution.py:54
  87.2 106.7 %copy-start.4 = (s32[512]{0:T(512)S(1)}, s32[512]{0:T(512)}, u32[]{:S(2)}) copy-start(s32[512]{0:T(512)} %param.13) | copy-start | bytes 6148
  193.9 40.7 %copy-start = (f32[512]{0:T(512)S(1)}, f32[512]{0:T(512)}, u32[]{:S(2)}) copy-start(f32[512]{0:T(512)} %param.16) | copy-start | bytes 6148
  193.9 40.7 %copy-start.1 = (s32[512]{0:T(512)S(1)}, s32[512]{0:T(512)}, u32[]{:S(2)}) copy-start(s32[512]{0:T(512)} %param.15) | copy-start | bytes 6148
  193.9 40.7 %copy-start.2 = (f32[512]{0:T(512)S(1)}, f32[512]{0:T(512)}, u32[]{:S(2)}) copy-start(f32[512]{0:T(512)} %param.14) | copy-start | bytes 6148
  193.9 40.7 %copy-start.3 = (s32[512]{0:T(512)S(1)}, s32[512]{0:T(512)}, u32[]{:S(2)}) copy-start(s32[512]{0:T(512)} %param.17) | copy-start | bytes 6148
Sparse Core Ops, SparseCore 0:
  10.9 67.9 all-gather.2
  81.7 64.1 all-gather.4
where the time goes:
time: 433 us
  blocking collectives  258 us (60%)
  waiting for transfers between devices  130 us (30%)
  matrix products  27 us (6%)
  between operations  14.1 us (3%)
    psum x1, blocking collectives, shards(): summed = lax.psum(partial_grad, 'vocab')  179 us
    all_gather x1, waiting for transfers between devices, shards(): lax.all_gather(policy_hidden, 'vocab', axis=0, tiled=True)  70.2 us
    all_gather x1, waiting for transfers between devices, shards(): lax.all_gather(frozen_hidden, 'vocab', axis=0, tiled=True)  58.7 us
    pmax x1, blocking collectives, shards(): policy_peak, frozen_peak = lax.pmax((policy_local, frozen_local), 'vocab')  39.7 us
    psum x1, blocking collectives, shards(): lax.psum((sums_here[0], sums_here[1], sums_here[2], sums_here[3]), 'vocab')  39.6 us
    dot_general x2, matrix products, head_product(): lax.dot_general(rows_block, head, (((1,), (1,)), ((), ())), preferred_ele...  16.6 us
    dot_general x1, matrix products, shards(): jnp.dot(logit_grad, policy_head, preferred_element_type=jnp.float32)  10.4 us
  transfers between devices with their start and end apart: 2, of which 2 were waited for; matrix products, arithmetic and copies ran while one was open for 2% of the time, Pallas kernels for 0%

commit v1 on v0

--- a/solution.py
+++ b/solution.py
@@ -1,6 +1,8 @@
 import jax
 import jax.numpy as jnp
 from jax import lax
+from jax.experimental import pallas as pl
+from jax.experimental.pallas import tpu as pltpu
 from jax.sharding import PartitionSpec as P
 
 clip_eps = 0.2
@@ -86,6 +88,468 @@
     return (hidden_grad.astype(jnp.bfloat16), surrogate_loss)
 
 
+MESH = pl.DeviceIdType.MESH
+f32 = jnp.float32
+bf16 = jnp.bfloat16
+GATHER = ((0, 0, "zxy"), (0, 1, "zyx"), (1, 0, "xzy"), (1, 1, "yzx"))
+SCATTER = ("yxz", "xyz", "yzx", "xzy")
+
+
+def nt_dot(a, b):
+    return lax.dot_general(a, b, (((1,), (1,)), ((), ())), preferred_element_type=f32)
+
+
+def gather_events():
+    events = []
+    for part, (_, _, order) in enumerate(GATHER):
+        for dz in range(-3, 4):
+            for dy in range(2):
+                for dx in range(2):
+                    moved = {"z": dz, "y": dy, "x": dx}
+                    last = max([order.index(a) for a in order if moved[a]], default=-1)
+                    onward = order[last + 1 :]
+                    depth = abs(dz) + dy + dx
+                    events.append((depth, part, dz, dy, dx, order[last] if last >= 0 else "", onward))
+    events.sort(key=lambda e: (e[0], e[1]))
+    return events
+
+
+def kernel(
+    ph, fh, pw_hbm, fw_hbm, act, beh, sgn, siz, msk,
+    out, loss,
+    hid, pw, fw, pl_acc, fl_acc, cols, rows, grad, st1, st2,
+    sib_out, sib_in, acc, s1, r1, s2, r2, zs, zr,
+    load_sem, g_send, g_recv, g_sib, st_send, st_recv, st2_send, st2_recv,
+    sib_send, sib_recv, s1_send, s1_recv, s2_send, s2_recv, z_send, z_recv,
+):
+    tokens, vocab_rows = pl_acc.shape
+    width = ph.shape[1]
+    half, quarter = width // 2, width // 4
+    me = lax.axis_index("vocab")
+    c, x, y, z = me % 2, (me // 2) % 2, (me // 4) % 2, me // 8
+    plane = me % 8
+
+    def dev(zz, yy, xx, cc):
+        return {"vocab": ((zz * 2 + yy) * 2 + xx) * 2 + cc}
+
+    sibling = dev(z, y, x, 1 - c)
+
+    def put(src, dst, send, recv, where):
+        return pltpu.make_async_remote_copy(
+            src_ref=src, dst_ref=dst, send_sem=send, recv_sem=recv,
+            device_id=where, device_id_type=MESH,
+        )
+
+    load_p = pltpu.make_async_copy(pw_hbm, pw, load_sem.at[0])
+    load_f = pltpu.make_async_copy(fw_hbm, fw, load_sem.at[1])
+    load_p.start()
+    load_f.start()
+    barrier = pltpu.get_barrier_semaphore()
+    for k in range(1, 8):
+        pl.semaphore_signal(
+            barrier, inc=1, device_id={"vocab": z * 8 + (plane + k) % 8}, device_id_type=MESH
+        )
+    for k in range(1, 4):
+        pl.semaphore_signal(
+            barrier, inc=1, device_id={"vocab": ((z + k) % 4) * 8 + plane}, device_id_type=MESH
+        )
+    hid[0, z, y, x, c] = ph[...]
+    hid[1, z, y, x, c] = fh[...]
+    pl.semaphore_wait(barrier, 10)
+
+    def chunk(part, sz, sy, sx, sc):
+        model, side, _ = GATHER[part]
+        return hid.at[model, sz, sy, sx, sc, :, pl.ds(side * half, half)]
+
+    def gather_copy(part, sz, sy, sx, way):
+        where, slot = {
+            "+": (dev(z + 1, y, x, c), 0),
+            "-": (dev(z - 1, y, x, c), 1),
+            "y": (dev(z, 1 - y, x, c), 2),
+            "x": (dev(z, y, 1 - x, c), 3),
+            "s": (sibling, 4),
+        }[way]
+        source = (sz * 2 + sy) * 2 + sx
+        block = chunk(part, sz, sy, sx, c)
+        if way == "s":
+            _, _, order = GATHER[part]
+            recv = g_sib.at[part, source]
+        else:
+            recv = g_recv.at[part, source]
+        return put(block, block, g_send.at[part, source, slot], recv, where)
+
+    def gather_event(event, act_on):
+        _, part, dz, dy, dx, last, onward = event
+        sz, sy, sx = z + dz, (1 - y if dy else y), (1 - x if dx else x)
+
+        def go():
+            if act_on == "start" and last:
+                gather_copy(part, sz, sy, sx, "y").wait_recv()
+
+            def each(way, cond=None):
+                def run():
+                    copy = gather_copy(part, sz, sy, sx, way)
+                    if act_on == "start":
+                        copy.start()
+                    else:
+                        copy.wait_send()
+
+                if cond is None:
+                    run()
+                else:
+                    pl.when(cond)(run)
+
+            if ("z" in onward and dz == 0) or (last == "z" and dz < 0):
+                each("+", z < 3)
+            if ("z" in onward and dz == 0) or (last == "z" and dz > 0):
+                each("-", z > 0)
+            for way in onward:
+                if way != "z":
+                    each(way)
+            each("s")
+
+        if dz == 0:
+            go()
+        else:
+            pl.when((sz >= 0) & (sz <= 3))(go)
+
+    events = gather_events()
+    for event in events:
+        gather_event(event, "start")
+        if event[0] == 0 and event[1] == 3:
+            rows[...] = jnp.zeros_like(rows)
+            rows[0:1, :] = act[...].astype(f32)
+            for b in range(tokens // 128):
+                span = pl.ds(b * 128, 128)
+                cols[span, :] = rows[:, span].T
+
+    def wait_sibling(part):
+        @pl.loop(0, 16)
+        def _(i):
+            block = chunk(part, i // 4, (i // 2) % 2, i % 2, 1 - c)
+            put(block, block, g_send.at[part, 0, 4], g_sib.at[part, i], sibling).wait_recv()
+
+    load_p.wait()
+    load_f.wait()
+    tile = half // 2
+    for part, (model, side, _) in enumerate(GATHER):
+        wait_sibling(part)
+        head, total = (pw, pl_acc) if model == 0 else (fw, fl_acc)
+
+        @pl.loop(0, 2)
+        def _(i):
+            span = pl.ds(pl.multiple_of(side * half + i * tile, tile), tile)
+            new = nt_dot(hid[model, :, :, :, :, :, span].reshape(tokens, tile), head[:, span])
+            if side == 0:
+                @pl.when(i == 0)
+                def _():
+                    total[...] = new
+
+                @pl.when(i > 0)
+                def _():
+                    total[...] += new
+            else:
+                total[...] += new
+
+    block_rows = 128
+    first = (me * vocab_rows).astype(f32)
+
+    def chosen_of(span):
+        ids = lax.broadcasted_iota(jnp.int32, (block_rows, vocab_rows), 1).astype(f32) + first
+        return cols[span, 0:1] == ids
+
+    for b in range(tokens // block_rows):
+        span = pl.ds(b * block_rows, block_rows)
+        pol, fro = pl_acc[span, :], fl_acc[span, :]
+        ppk = jnp.max(pol, axis=1, keepdims=True)
+        fpk = jnp.max(fro, axis=1, keepdims=True)
+        ex = jnp.exp(pol - ppk)
+        stats = (
+            ppk,
+            jnp.sum(ex, axis=1, keepdims=True),
+            jnp.sum(ex * (pol - fro), axis=1, keepdims=True),
+            fpk,
+            jnp.sum(jnp.exp(fro - fpk), axis=1, keepdims=True),
+            jnp.sum(jnp.where(chosen_of(span), pol, 0.0), axis=1, keepdims=True),
+        )
+        lane = lax.broadcasted_iota(jnp.int32, (block_rows, 128), 1)
+        packed = jnp.zeros((block_rows, 128), f32)
+        for i, s in enumerate(stats):
+            packed = jnp.where(lane == i, s, packed)
+        st1[plane, :, b * block_rows : (b + 1) * block_rows] = packed.T[0:8, :]
+
+    def combine(blocks):
+        ppk, fpk = blocks[0][0:1], blocks[0][3:4]
+        for blk in blocks[1:]:
+            ppk, fpk = jnp.maximum(ppk, blk[0:1]), jnp.maximum(fpk, blk[3:4])
+        pt = gap = ft = pick = 0.0
+        for blk in blocks:
+            scale = jnp.exp(blk[0:1] - ppk)
+            pt = pt + scale * blk[1:2]
+            gap = gap + scale * blk[2:3]
+            ft = ft + jnp.exp(blk[3:4] - fpk) * blk[4:5]
+            pick = pick + blk[5:6]
+        return ppk, pt, gap, fpk, ft, pick
+
+    def st1_copy(k, slot):
+        where = {"vocab": z * 8 + (plane + k) % 8}
+        return put(st1.at[slot], st1.at[slot], st_send.at[k], st_recv.at[slot], where)
+
+    def st2_copy(k, slot):
+        where = {"vocab": ((z + k) % 4) * 8 + plane}
+        return put(st2.at[slot], st2.at[slot], st2_send.at[k], st2_recv.at[slot], where)
+
+    for k in range(1, 8):
+        st1_copy(k, plane).start()
+    for event in events:
+        gather_event(event, "finish")
+    for k in range(1, 8):
+        st1_copy(k, (plane + k) % 8).wait_recv()
+    both = combine([st1[i] for i in range(8)])
+    for i, s in enumerate(both):
+        st2[z, i : i + 1, :] = s
+    st2[z, 6:8, :] = jnp.zeros((2, tokens), f32)
+    for k in range(1, 4):
+        st2_copy(k, z).start()
+    for k in range(1, 4):
+        st2_copy(k, (z + k) % 4).wait_recv()
+    ppk, pt, gap, fpk, ft, picked = combine([st2[i] for i in range(4)])
+
+    policy_lse = ppk + jnp.log(pt)
+    frozen_lse = fpk + jnp.log(ft)
+    gap_mean = gap / pt
+    divergence = gap_mean - policy_lse + frozen_lse
+    objective, slope = surrogate(picked - policy_lse, beh[...], sgn[...], siz[...])
+    weight = msk[...].astype(f32)
+    loss[...] = jnp.sum(weight * (objective + kl_weight * divergence), axis=1, keepdims=True)
+    rows[1:2, :] = policy_lse
+    rows[2:3, :] = gap_mean
+    rows[3:4, :] = slope
+    rows[4:5, :] = loss_scale * weight
+    for b in range(tokens // block_rows):
+        span = pl.ds(b * block_rows, block_rows)
+        cols[span, :] = rows[:, span].T
+        pol, fro = pl_acc[span, :], fl_acc[span, :]
+        prob = jnp.exp(pol - cols[span, 1:2])
+        value = cols[span, 4:5] * (
+            cols[span, 3:4] * (chosen_of(span).astype(f32) - prob)
+            + kl_weight * prob * ((pol - fro) - cols[span, 2:3])
+        )
+        grad[pl.ds(b * 4, 4)] = value.astype(bf16).reshape(4, 2, 16, vocab_rows)
+
+    def product(core, q):
+        left = grad[:, core].reshape(tokens // 2, vocab_rows)
+        right = pw[:, q * quarter : (q + 1) * quarter]
+        made = jnp.dot(left, right, preferred_element_type=f32)
+        return made.reshape(4, 2, 2, 16, quarter)
+
+    def sib_copy(q):
+        return put(sib_out.at[q], sib_in.at[q], sib_send.at[q], sib_recv.at[q], sibling)
+
+    for q in range(4):
+        sib_out[q] = product(1 - c, q).astype(bf16)
+        sib_copy(q).start()
+
+    flip_x, flip_y = dev(z, y, 1 - x, c), dev(z, 1 - y, x, c)
+
+    def sides(q):
+        order = SCATTER[q]
+        own, other = (y, x) if order[0] == "y" else (x, y)
+        to_first, to_other = (flip_y, flip_x) if order[0] == "y" else (flip_x, flip_y)
+        return own, other, to_first, to_other
+
+    def s1_copy(q, zz):
+        _, _, to_first, _ = sides(q)
+        return put(s1.at[q, zz], r1.at[q, zz], s1_send.at[q, zz], s1_recv.at[q, zz], to_first)
+
+    def s2_copy(q, zz):
+        _, _, _, to_other = sides(q)
+        return put(s2.at[q, zz], r2.at[q, zz], s2_send.at[q, zz], s2_recv.at[q, zz], to_other)
+
+    def z_slot(ref, q, way, dest):
+        if SCATTER[q][2] == "z":
+            return ref.at[q, way, dest, 0]
+        return ref.at[q, way, dest]
+
+    def z_copy(q, way, dest):
+        where = dev(z + 1, y, x, c) if way == 0 else dev(z - 1, y, x, c)
+        return put(
+            z_slot(zs, q, way, dest), z_slot(zr, q, way, dest),
+            z_send.at[q, way, dest], z_recv.at[q, way, dest], where,
+        )
+
+    for q in range(4):
+        made = product(c, q)
+        sib_copy(q).wait_recv()
+        made = made + sib_in[q].astype(f32)
+        own, other, _, _ = sides(q)
+        for i in range(2):
+            for j in range(2):
+                acc[q, :, i, j] = made[:, i, j] if SCATTER[q][0] == "y" else made[:, j, i]
+        for zz in range(4):
+            s1[q, zz] = acc[q, zz, 1 - own].astype(bf16)
+            s1_copy(q, zz).start()
+
+    def take_first(q, zz):
+        own, _, _, _ = sides(q)
+        s1_copy(q, zz).wait_recv()
+        acc[q, zz, own] += r1[q, zz].astype(f32)
+
+    for zz in range(4):
+        for q in range(4):
+            own, other, _, _ = sides(q)
+            take_first(q, zz)
+            if SCATTER[q][2] == "z":
+                s2[q, zz] = acc[q, zz, own, 1 - other].astype(bf16)
+                s2_copy(q, zz).start()
+
+    def line_value(q, dest):
+        own, other, _, _ = sides(q)
+        if SCATTER[q][2] == "z":
+            return acc.at[q, dest, own, other]
+        return acc.at[q, dest, own]
+
+    def line_step(q, k):
+        @pl.when(z + k <= 3)
+        def _():
+            dest = z + k
+            held = line_value(q, dest)
+
+            @pl.when(z > 0)
+            def _():
+                z_copy(q, 0, dest).wait_recv()
+                held[...] += z_slot(zr, q, 0, dest)[...].astype(f32)
+
+            z_slot(zs, q, 0, dest)[...] = held[...].astype(bf16)
+            z_copy(q, 0, dest).start()
+
+        @pl.when(z - k >= 0)
+        def _():
+            dest = z - k
+            held = line_value(q, dest)
+
+            @pl.when(z < 3)
+            def _():
+                z_copy(q, 1, dest).wait_recv()
+                held[...] += z_slot(zr, q, 1, dest)[...].astype(f32)
+
+            z_slot(zs, q, 1, dest)[...] = held[...].astype(bf16)
+            z_copy(q, 1, dest).start()
+
+    def line_end(q):
+        held = line_value(q, z)
+
+        @pl.when(z > 0)
+        def _():
+            z_copy(q, 0, z).wait_recv()
+            held[...] += z_slot(zr, q, 0, z)[...].astype(f32)
+
+        @pl.when(z < 3)
+        def _():
+            z_copy(q, 1, z).wait_recv()
+            held[...] += z_slot(zr, q, 1, z)[...].astype(f32)
+
+    for k in (3, 2, 1):
+        for q in (2, 3):
+            line_step(q, k)
+    for q in (2, 3):
+        line_end(q)
+        own, other, _, _ = sides(q)
+        s2[q, 0] = acc[q, z, own, 1 - other].astype(bf16)
+        s2_copy(q, 0).start()
+    for q in (0, 1):
+        own, other, _, _ = sides(q)
+        for zz in range(4):
+            s2_copy(q, zz).wait_recv()
+            acc[q, zz, own, other] += r2[q, zz].astype(f32)
+    for k in (3, 2, 1):
+        for q in (0, 1):
+            line_step(q, k)
+    for q in (2, 3):
+        own, other, _, _ = sides(q)
+        s2_copy(q, 0).wait_recv()
+        done = acc[q, z, own, other] + r2[q, 0].astype(f32)
+        out[:, q * quarter : (q + 1) * quarter] = done.astype(bf16)
+    for q in (0, 1):
+        own, other, _, _ = sides(q)
+        line_end(q)
+        out[:, q * quarter : (q + 1) * quarter] = acc[q, z, own, other].astype(bf16)
+
+    for k in range(1, 8):
+        st1_copy(k, plane).wait_send()
+    for k in range(1, 4):
+        st2_copy(k, z).wait_send()
+    for q in range(4):
+        sib_copy(q).wait_send()
+        for zz in range(4):
+            s1_copy(q, zz).wait_send()
+        for zz in range(4 if SCATTER[q][2] == "z" else 1):
+            s2_copy(q, zz).wait_send()
+        for k in (3, 2, 1):
+            @pl.when(z + k <= 3)
+            def _():
+                z_copy(q, 0, z + k).wait_send()
+
+            @pl.when(z - k >= 0)
+            def _():
+                z_copy(q, 1, z - k).wait_send()
+
+
+def fused(ph, fh, pw, fw, actions, behavior, sign, size, mask):
+    own_rows, width = ph.shape
+    vocab_rows = pw.shape[0]
+    tokens = actions.shape[0]
+    quarter = width // 4
+    vmem, dma = pltpu.VMEM, pltpu.SemaphoreType.DMA
+    row = lambda a: a.reshape(1, tokens)
+    in_vmem = pl.BlockSpec(memory_space=pltpu.VMEM)
+    in_hbm = pl.BlockSpec(memory_space=pl.ANY)
+    out, loss = pl.pallas_call(
+        kernel,
+        out_shape=(
+            jax.ShapeDtypeStruct((own_rows, width), bf16),
+            jax.ShapeDtypeStruct((1, 1), f32),
+        ),
+        in_specs=[in_vmem, in_vmem, in_hbm, in_hbm] + [in_vmem] * 5,
+        out_specs=(in_vmem, in_vmem),
+        scratch_shapes=[
+            vmem((2, 4, 2, 2, 2, own_rows, width), bf16),
+            vmem((vocab_rows, width), bf16),
+            vmem((vocab_rows, width), bf16),
+            vmem((tokens, vocab_rows), f32),
+            vmem((tokens, vocab_rows), f32),
+            vmem((tokens, 128), f32),
+            vmem((128, tokens), f32),
+            vmem((16, 2, own_rows, vocab_rows), bf16),
+            vmem((8, 8, tokens), f32),
+            vmem((4, 8, tokens), f32),
+            vmem((4, 4, 2, 2, own_rows, quarter), bf16),
+            vmem((4, 4, 2, 2, own_rows, quarter), bf16),
+            vmem((4, 4, 2, 2, own_rows, quarter), f32),
+            vmem((4, 4, 2, own_rows, quarter), bf16),
+            vmem((4, 4, 2, own_rows, quarter), bf16),
+            vmem((4, 4, own_rows, quarter), bf16),
+            vmem((4, 4, own_rows, quarter), bf16),
+            vmem((4, 2, 4, 2, own_rows, quarter), bf16),
+            vmem((4, 2, 4, 2, own_rows, quarter), bf16),
+            dma((2,)), dma((4, 16, 5)), dma((4, 16)), dma((4, 16)),
+            dma((8,)), dma((8,)), dma((4,)), dma((4,)),
+            dma((4,)), dma((4,)), dma((4, 4)), dma((4, 4)),
+            dma((4, 4)), dma((4, 4)), dma((4, 2, 4)), dma((4, 2, 4)),
+        ],
+        compiler_params=pltpu.CompilerParams(
+            collective_id=0, has_side_effects=True, vmem_limit_bytes=60 * 1024 * 1024
+        ),
+        cost_estimate=pl.CostEstimate(
+            flops=6 * tokens * width * vocab_rows,
+            bytes_accessed=4 * width * vocab_rows,
+            transcendentals=3 * tokens * vocab_rows,
+        ),
+        name="fused",
+    )(ph, fh, pw, fw, row(actions), row(behavior), row(sign), row(size), row(mask))
+    return out, loss.reshape(1)
+
+
 def solution(mesh):
     placed = (
         P(("groups", "vocab"), None),
@@ -98,8 +562,9 @@
         P("groups"),
         P("groups"),
     )
+    body = fused if dict(mesh.shape) == {"groups": 1, "vocab": 32} else shards
     return jax.shard_map(
-        shards,
+        body,
         mesh=mesh,
         in_specs=placed,
         out_specs=(P(("groups", "vocab"), None), P("groups")),

time: 433 us -> 123 us (0.28)
  blocking collectives: 258 us -> 0 us
  waiting for transfers between devices: 130 us -> 0 us
  Pallas kernels: 0 us -> 119 us
  matrix products: 27 us -> 0 us
  between operations: 14.1 us -> 2.4 us
    psum x2 -> x0, blocking collectives: 218 us -> none  [the longest x1 179 us: shards(): summed = lax.psum(partial_grad, 'vocab')]
    all_gather x2 -> x0, waiting for transfers between devices: 129 us -> none  [the longest x1 70.2 us: shards(): lax.all_gather(policy_hidden, 'vocab', axis=0, tiled=True)]
    pallas_call x0 -> x1, Pallas kernels: none -> 119 us  [fused(): pl.pallas_call(kernel, out_shape=(jax.ShapeDtypeStruct((own_rows, width),...]
    pmax x1 -> x0, blocking collectives: 39.7 us -> none  [shards(): policy_peak, frozen_peak = lax.pmax((policy_local, frozen_local), 'vocab')]
    dot_general x3 -> x0, matrix products: 27 us -> none  [the longest x2 16.6 us: head_product(): lax.dot_general(rows_block, head, (((1,), (1,)), ((), ())), preferred_ele...]
  transfers between devices with their start and end apart: 2 -> 0, of which waited for: 2 -> 0; matrix products, arithmetic and copies ran while one was open for 2% -> 0% of each run, Pallas kernels for 0% -> 0%
where the time goes in v1:
time: 123 us
  Pallas kernels  119 us (97%)
  between operations  2.4 us (2%)
  local copies, waits for them, and re-layouts  1.59 us (1%)
    pallas_call x1, Pallas kernels, fused(): pl.pallas_call(kernel, out_shape=(jax.ShapeDtypeStruct((own_rows, width),...  119 us

profile of v1, /device:TPU:0, one launch (start us, length us, event | category | flops | bytes accessed | tf_op | source)
XLA Modules:
  0.0 122.9 jit_solution(18309048711849031592)
XLA Ops:
  0.6 118.9 %fused.1 = (bf16[16,5120]{1,0:T(8,128)(2,1)}, f32[1,1]{1,0:T(1,128)}) custom-call(bf16[16,5120]{1,0:T(8,128)(2,1)} %ph.1, bf16[16,5120]{1,0:T(8,128)(2,1)} %fh.1, bf16[640,5120]{1,0:T(8,128)(2,1)} %pw_hbm.1, bf16[640,5120]{1,0:T(8,128)(2,1)} %fw_hbm.1, s32[1,512]{1,0:T(1,128)} %bitcast.6, f32[1,512]{1,0:T(1,128)} %bitcast.7, s32[1,512]{1,0:T(1,128)} %bitcast.8, ...), custom_call_target="tpu_custom_call" | custom-call | flops 10066329600 | bytes 13107200 | tf_op jit(solution)/shard_map/fused/pallas_call | solution.py:507
  119.6 1.6 %copy.13 = bf16[16,5120]{1,0:T(8,128)(2,1)} copy(bf16[16,5120]{1,0:T(8,128)(2,1)} %get-tuple-element.8) | data formatting | bytes 327680

commit v2 on v1

--- a/solution.py
+++ b/solution.py
@@ -109,8 +109,9 @@
                     last = max([order.index(a) for a in order if moved[a]], default=-1)
                     onward = order[last + 1 :]
                     depth = abs(dz) + dy + dx
-                    events.append((depth, part, dz, dy, dx, order[last] if last >= 0 else "", onward))
-    events.sort(key=lambda e: (e[0], e[1]))
+                    late = moved[order[2]]
+                    events.append((depth, part, dz, dy, dx, order[last] if last >= 0 else "", onward, late))
+    events.sort(key=lambda e: (e[0], e[7], e[1]))
     return events
 
 
@@ -122,7 +123,7 @@
     load_sem, g_send, g_recv, g_sib, st_send, st_recv, st2_send, st2_recv,
     sib_send, sib_recv, s1_send, s1_recv, s2_send, s2_recv, z_send, z_recv,
 ):
-    tokens, vocab_rows = pl_acc.shape
+    tokens, vocab_rows = cols.shape[0], pw.shape[0]
     width = ph.shape[1]
     half, quarter = width // 2, width // 4
     me = lax.axis_index("vocab")
@@ -153,6 +154,8 @@
         pl.semaphore_signal(
             barrier, inc=1, device_id={"vocab": ((z + k) % 4) * 8 + plane}, device_id_type=MESH
         )
+    pl_acc[...] = jnp.zeros_like(pl_acc)
+    fl_acc[...] = jnp.zeros_like(fl_acc)
     hid[0, z, y, x, c] = ph[...]
     hid[1, z, y, x, c] = fh[...]
     pl.semaphore_wait(barrier, 10)
@@ -179,7 +182,7 @@
         return put(block, block, g_send.at[part, source, slot], recv, where)
 
     def gather_event(event, act_on):
-        _, part, dz, dy, dx, last, onward = event
+        _, part, dz, dy, dx, last, onward, _ = event
         sz, sy, sx = z + dz, (1 - y if dy else y), (1 - x if dx else x)
 
         def go():
@@ -213,8 +216,39 @@
         else:
             pl.when((sz >= 0) & (sz <= 3))(go)
 
+    def wait_sibling(part, far):
+        _, _, order = GATHER[part]
+
+        @pl.loop(0, 8)
+        def _(i):
+            sz, j = i // 2, i % 2
+            if order[2] == "y":
+                sy, sx = (1 - y if far else y), j
+            else:
+                sy, sx = j, (1 - x if far else x)
+            block = chunk(part, sz, sy, sx, 1 - c)
+            source = (sz * 2 + sy) * 2 + sx
+            put(block, block, g_send.at[part, 0, 4], g_sib.at[part, source], sibling).wait_recv()
+
+    tile = half // 2
+
+    def logits_piece(part, far, i):
+        model, side, order = GATHER[part]
+        head, total = (pw, pl_acc) if model == 0 else (fw, fl_acc)
+        span = pl.ds(side * half + i * tile, tile)
+        shape = (4, 2, 2, 16, vocab_rows)
+        if order[2] == "y":
+            at = 1 - y if far else y
+            left = hid[model, :, at, :, :, :, span].reshape(tokens // 2, tile)
+            total[:, at] += nt_dot(left, head[:, span]).reshape(shape)
+        else:
+            at = 1 - x if far else x
+            left = hid[model, :, :, at, :, :, span].reshape(tokens // 2, tile)
+            total[:, :, at] += nt_dot(left, head[:, span]).reshape(shape)
+
     events = gather_events()
-    for event in events:
+    cut = max(i for i, e in enumerate(events) if not e[7]) + 1
+    for event in events[:cut]:
         gather_event(event, "start")
         if event[0] == 0 and event[1] == 3:
             rows[...] = jnp.zeros_like(rows)
@@ -222,34 +256,21 @@
             for b in range(tokens // 128):
                 span = pl.ds(b * 128, 128)
                 cols[span, :] = rows[:, span].T
-
-    def wait_sibling(part):
-        @pl.loop(0, 16)
-        def _(i):
-            block = chunk(part, i // 4, (i // 2) % 2, i % 2, 1 - c)
-            put(block, block, g_send.at[part, 0, 4], g_sib.at[part, i], sibling).wait_recv()
-
     load_p.wait()
     load_f.wait()
-    tile = half // 2
-    for part, (model, side, _) in enumerate(GATHER):
-        wait_sibling(part)
-        head, total = (pw, pl_acc) if model == 0 else (fw, fl_acc)
-
-        @pl.loop(0, 2)
-        def _(i):
-            span = pl.ds(pl.multiple_of(side * half + i * tile, tile), tile)
-            new = nt_dot(hid[model, :, :, :, :, :, span].reshape(tokens, tile), head[:, span])
-            if side == 0:
-                @pl.when(i == 0)
-                def _():
-                    total[...] = new
-
-                @pl.when(i > 0)
-                def _():
-                    total[...] += new
-            else:
-                total[...] += new
+    left_over = events[cut:]
+    pieces = [(part, i) for part in range(4) for i in range(2)]
+    step = -(-len(left_over) // len(pieces))
+    for n, (part, i) in enumerate(pieces):
+        if i == 0:
+            wait_sibling(part, False)
+        logits_piece(part, False, i)
+        for event in left_over[n * step : (n + 1) * step]:
+            gather_event(event, "start")
+    for part, i in pieces:
+        if i == 0:
+            wait_sibling(part, True)
+        logits_piece(part, True, i)
 
     block_rows = 128
     first = (me * vocab_rows).astype(f32)
@@ -260,7 +281,8 @@
 
     for b in range(tokens // block_rows):
         span = pl.ds(b * block_rows, block_rows)
-        pol, fro = pl_acc[span, :], fl_acc[span, :]
+        pol = pl_acc[b].reshape(block_rows, vocab_rows)
+        fro = fl_acc[b].reshape(block_rows, vocab_rows)
         ppk = jnp.max(pol, axis=1, keepdims=True)
         fpk = jnp.max(fro, axis=1, keepdims=True)
         ex = jnp.exp(pol - ppk)
@@ -329,7 +351,8 @@
     for b in range(tokens // block_rows):
         span = pl.ds(b * block_rows, block_rows)
         cols[span, :] = rows[:, span].T
-        pol, fro = pl_acc[span, :], fl_acc[span, :]
+        pol = pl_acc[b].reshape(block_rows, vocab_rows)
+        fro = fl_acc[b].reshape(block_rows, vocab_rows)
         prob = jnp.exp(pol - cols[span, 1:2])
         value = cols[span, 4:5] * (
             cols[span, 3:4] * (chosen_of(span).astype(f32) - prob)
@@ -346,7 +369,7 @@
     def sib_copy(q):
         return put(sib_out.at[q], sib_in.at[q], sib_send.at[q], sib_recv.at[q], sibling)
 
-    for q in range(4):
+    def for_sibling(q):
         sib_out[q] = product(1 - c, q).astype(bf16)
         sib_copy(q).start()
 
@@ -367,8 +390,6 @@
         return put(s2.at[q, zz], r2.at[q, zz], s2_send.at[q, zz], s2_recv.at[q, zz], to_other)
 
     def z_slot(ref, q, way, dest):
-        if SCATTER[q][2] == "z":
-            return ref.at[q, way, dest, 0]
         return ref.at[q, way, dest]
 
     def z_copy(q, way, dest):
@@ -378,7 +399,7 @@
             z_send.at[q, way, dest], z_recv.at[q, way, dest], where,
         )
 
-    for q in range(4):
+    def for_own(q):
         made = product(c, q)
         sib_copy(q).wait_recv()
         made = made + sib_in[q].astype(f32)
@@ -390,23 +411,25 @@
             s1[q, zz] = acc[q, zz, 1 - own].astype(bf16)
             s1_copy(q, zz).start()
 
+    for_sibling(2)
+    for_sibling(3)
+    for_own(2)
+    for_sibling(0)
+    for_own(3)
+    for_sibling(1)
+    for_own(0)
+    for_own(1)
+
     def take_first(q, zz):
-        own, _, _, _ = sides(q)
+        own, other, _, _ = sides(q)
         s1_copy(q, zz).wait_recv()
         acc[q, zz, own] += r1[q, zz].astype(f32)
-
-    for zz in range(4):
-        for q in range(4):
-            own, other, _, _ = sides(q)
-            take_first(q, zz)
-            if SCATTER[q][2] == "z":
-                s2[q, zz] = acc[q, zz, own, 1 - other].astype(bf16)
-                s2_copy(q, zz).start()
+        if SCATTER[q][2] == "z":
+            s2[q, zz] = acc[q, zz, own, 1 - other].astype(bf16)
+            s2_copy(q, zz).start()
 
     def line_value(q, dest):
-        own, other, _, _ = sides(q)
-        if SCATTER[q][2] == "z":
-            return acc.at[q, dest, own, other]
+        own, _, _, _ = sides(q)
         return acc.at[q, dest, own]
 
     def line_step(q, k):
@@ -449,22 +472,38 @@
             z_copy(q, 1, z).wait_recv()
             held[...] += z_slot(zr, q, 1, z)[...].astype(f32)
 
+    def direct_copy(q, dest, slot):
+        return put(
+            zs.at[q, 0, dest, 0], zr.at[q, 0, slot, 0],
+            z_send.at[q, 0, dest], z_recv.at[q, 0, slot], dev(dest, y, x, c),
+        )
+
+    for zz in range(4):
+        for q in (2, 3):
+            take_first(q, zz)
     for k in (3, 2, 1):
         for q in (2, 3):
             line_step(q, k)
+        for q in (0, 1):
+            take_first(q, 3 - k)
     for q in (2, 3):
         line_end(q)
         own, other, _, _ = sides(q)
         s2[q, 0] = acc[q, z, own, 1 - other].astype(bf16)
         s2_copy(q, 0).start()
     for q in (0, 1):
-        own, other, _, _ = sides(q)
-        for zz in range(4):
+        take_first(q, 3)
+    for zz in range(4):
+        for q in (0, 1):
+            own, other, _, _ = sides(q)
             s2_copy(q, zz).wait_recv()
             acc[q, zz, own, other] += r2[q, zz].astype(f32)
-    for k in (3, 2, 1):
-        for q in (0, 1):
-            line_step(q, k)
+
+            @pl.when(z != zz)
+            def _():
+                zs[q, 0, zz, 0] = acc[q, zz, own, other].astype(bf16)
+                direct_copy(q, zz, z).start()
+
     for q in (2, 3):
         own, other, _, _ = sides(q)
         s2_copy(q, 0).wait_recv()
@@ -472,8 +511,12 @@
         out[:, q * quarter : (q + 1) * quarter] = done.astype(bf16)
     for q in (0, 1):
         own, other, _, _ = sides(q)
-        line_end(q)
-        out[:, q * quarter : (q + 1) * quarter] = acc[q, z, own, other].astype(bf16)
+        done = acc[q, z, own, other]
+        for k in range(1, 4):
+            source = (z + k) % 4
+            direct_copy(q, source, source).wait_recv()
+            done = done + zr[q, 0, source, 0].astype(f32)
+        out[:, q * quarter : (q + 1) * quarter] = done.astype(bf16)
 
     for k in range(1, 8):
         st1_copy(k, plane).wait_send()
@@ -485,6 +528,10 @@
             s1_copy(q, zz).wait_send()
         for zz in range(4 if SCATTER[q][2] == "z" else 1):
             s2_copy(q, zz).wait_send()
+        if SCATTER[q][2] == "z":
+            for k in range(1, 4):
+                direct_copy(q, (z + k) % 4, z).wait_send()
+            continue
         for k in (3, 2, 1):
             @pl.when(z + k <= 3)
             def _():
@@ -516,8 +563,8 @@
             vmem((2, 4, 2, 2, 2, own_rows, width), bf16),
             vmem((vocab_rows, width), bf16),
             vmem((vocab_rows, width), bf16),
-            vmem((tokens, vocab_rows), f32),
-            vmem((tokens, vocab_rows), f32),
+            vmem((4, 2, 2, 2, own_rows, vocab_rows), f32),
+            vmem((4, 2, 2, 2, own_rows, vocab_rows), f32),
             vmem((tokens, 128), f32),
             vmem((128, tokens), f32),
             vmem((16, 2, own_rows, vocab_rows), bf16),

time: 123 us -> 109 us (0.89)
  Pallas kernels: 119 us -> 105 us
    pallas_call x1, Pallas kernels: 119 us -> 105 us  [fused(): pl.pallas_call(kernel, out_shape=(jax.ShapeDtypeStruct((own_rows, width),...]
where the time goes in v2:
time: 109 us
  Pallas kernels  105 us (96%)
  between operations  2.4 us (2%)
  local copies, waits for them, and re-layouts  1.59 us (1%)
    pallas_call x1, Pallas kernels, fused(): pl.pallas_call(kernel, out_shape=(jax.ShapeDtypeStruct((own_rows, width),...  105 us

profile of v2, /device:TPU:0, one launch (start us, length us, event | category | flops | bytes accessed | tf_op | source)
XLA Modules:
  0.0 108.7 jit_solution(16155515888364910121)
XLA Ops:
  0.6 104.7 %fused.1 = (bf16[16,5120]{1,0:T(8,128)(2,1)}, f32[1,1]{1,0:T(1,128)}) custom-call(bf16[16,5120]{1,0:T(8,128)(2,1)} %ph.1, bf16[16,5120]{1,0:T(8,128)(2,1)} %fh.1, bf16[640,5120]{1,0:T(8,128)(2,1)} %pw_hbm.1, bf16[640,5120]{1,0:T(8,128)(2,1)} %fw_hbm.1, s32[1,512]{1,0:T(1,128)} %bitcast.6, f32[1,512]{1,0:T(1,128)} %bitcast.7, s32[1,512]{1,0:T(1,128)} %bitcast.8, ...), custom_call_target="tpu_custom_call" | custom-call | flops 10066329600 | bytes 13107200 | tf_op jit(solution)/shard_map/fused/pallas_call | solution.py:554
  105.3 1.6 %copy.13 = bf16[16,5120]{1,0:T(8,128)(2,1)} copy(bf16[16,5120]{1,0:T(8,128)(2,1)} %get-tuple-element.8) | data formatting | bytes 327680

commit v3 on v2

--- a/solution.py
+++ b/solution.py
@@ -486,13 +486,13 @@
             line_step(q, k)
         for q in (0, 1):
             take_first(q, 3 - k)
+    for q in (0, 1):
+        take_first(q, 3)
     for q in (2, 3):
         line_end(q)
         own, other, _, _ = sides(q)
         s2[q, 0] = acc[q, z, own, 1 - other].astype(bf16)
         s2_copy(q, 0).start()
-    for q in (0, 1):
-        take_first(q, 3)
     for zz in range(4):
         for q in (0, 1):
             own, other, _, _ = sides(q)

time: 109 us -> 109 us (level)
  no operation moved by 1% of the time
where the time goes in v3:
time: 109 us
  Pallas kernels  105 us (96%)
  between operations  2.4 us (2%)
  local copies, waits for them, and re-layouts  1.59 us (1%)
    pallas_call x1, Pallas kernels, fused(): pl.pallas_call(kernel, out_shape=(jax.ShapeDtypeStruct((own_rows, width),...  105 us

profile of v3, /device:TPU:0, one launch (start us, length us, event | category | flops | bytes accessed | tf_op | source)
XLA Modules:
  0.0 108.6 jit_solution(6277627007142526842)
XLA Ops:
  0.6 104.6 %fused.1 = (bf16[16,5120]{1,0:T(8,128)(2,1)}, f32[1,1]{1,0:T(1,128)}) custom-call(bf16[16,5120]{1,0:T(8,128)(2,1)} %ph.1, bf16[16,5120]{1,0:T(8,128)(2,1)} %fh.1, bf16[640,5120]{1,0:T(8,128)(2,1)} %pw_hbm.1, bf16[640,5120]{1,0:T(8,128)(2,1)} %fw_hbm.1, s32[1,512]{1,0:T(1,128)} %bitcast.6, f32[1,512]{1,0:T(1,128)} %bitcast.7, s32[1,512]{1,0:T(1,128)} %bitcast.8, ...), custom_call_target="tpu_custom_call" | custom-call | flops 10066329600 | bytes 13107200 | tf_op jit(solution)/shard_map/fused/pallas_call | solution.py:554
  105.3 1.6 %copy.13 = bf16[16,5120]{1,0:T(8,128)(2,1)} copy(bf16[16,5120]{1,0:T(8,128)(2,1)} %get-tuple-element.8) | data formatting | bytes 327680
